TPU v7x, 128 devices: a whole 4x4x4 slice. The times are simulated.
128 devices in a mesh: grp: 4 (over y), seq: 32 (over x, z, core).
Axes of the slice: x: 4, y: 4, z: 4, core: 2. Of those that a mesh axis runs over, the one named last changes fastest.
Arguments:
- cand_x: bfloat16 [32768, 1024], P(('grp', 'seq')), may hold values from -6 to 6
- w_in: bfloat16 [1024, 4096], replicated, may hold values from -0.1875 to 0.1875
- w_out: bfloat16 [1024, 1024], P('grp'), may hold values from -0.1875 to 0.1875
- hist_keys: bfloat16 [4, 8192, 1024], P('grp', 'seq'), may hold values from -9 to 9
- hist_values: bfloat16 [4, 8192, 1024], P('grp', 'seq'), may hold values from -0.29882812 to 0.29882812
- hist_len: int32 [4], P('grp'), may hold values from 1024 to 8192, as said below
- cand_count: int32 [4], P('grp'), may hold values from 1024 to 8192, as said below
- panel_map: int32 [1024], P(('grp', 'seq')), may hold values from 0 to 255, as said below
Outputs:
- scored: bfloat16 [32768, 1024], P(('grp', 'seq'))
Inputs may be any that keep to these rules, and one draw needn't show every extreme that they name: `hist_len`: each user's lengths count its first events; one user has exactly 8192. `cand_count`: each user's real candidates are its candidate numbers below the count; one user has exactly 8192. `panel_map`: for each user, the 256 entries on the 32 devices of its group name every panel number once.
All inputs are finite; a program needn't handle non-finite values.
Results may differ from a plain program's by a relative error of at most 0.0055.
Values may be sent and summed in bfloat16 or wider, within the bound.
A program may use at most 192 MiB of HBM per device.

v0:
```python
import jax
import jax.numpy as jnp
from jax import lax
from jax.sharding import PartitionSpec as P

HEADS = 8
PANEL = 32


eps = 1e-06


def layer_norm(x):
    mean = jnp.mean(x, axis=-1, keepdims=True)
    var = jnp.mean((x - mean) ** 2, axis=-1, keepdims=True)
    return (x - mean) / jnp.sqrt(var + eps)


def attend(queries, keys, values, length):
    count, width = queries.shape
    head = width // HEADS
    events = keys.shape[0]
    scale = 1.0 / jnp.sqrt(jnp.float32(head))
    q_heads = queries.reshape(count, HEADS, head)
    k_heads = keys.reshape(events, HEADS, head)
    v_heads = values.reshape(events, HEADS, head)
    scores = (
        jnp.einsum("rhd,nhd->hrn", q_heads, k_heads, preferred_element_type=jnp.float32) * scale
    )
    positions = jnp.arange(events, dtype=jnp.int32)
    keep = positions < length
    weights = jnp.where(keep[None, None, :], jax.nn.silu(scores), 0.0).astype(jnp.bfloat16)
    summed = jnp.einsum("hrn,nhd->rhd", weights, v_heads, preferred_element_type=jnp.float32)
    return summed.reshape(count, width)


def per_device(cand_x, w_in, w_out, hist_keys, hist_values, hist_len, cand_count, panel_map):
    rows, width = cand_x.shape
    head = width // HEADS
    scale = 1.0 / jnp.sqrt(jnp.float32(head))
    length = hist_len[0]
    x32 = cand_x.astype(jnp.float32)
    normed = layer_norm(x32).astype(jnp.bfloat16)
    proj = jax.nn.silu(jnp.dot(normed, w_in, preferred_element_type=jnp.float32)).astype(
        jnp.bfloat16
    )
    u_part = proj[:, 0:width]
    v_part = proj[:, width : 2 * width]
    q_part = proj[:, 2 * width : 3 * width]
    k_part = proj[:, 3 * width : 4 * width]
    q_heads = q_part.astype(jnp.float32).reshape(rows, HEADS, head)
    k_heads = k_part.astype(jnp.float32).reshape(rows, HEADS, head)
    self_w = jax.nn.silu(jnp.sum(q_heads * k_heads, axis=-1) * scale).astype(jnp.bfloat16)
    self_term = (
        self_w.astype(jnp.float32)[:, :, None]
        * v_part.astype(jnp.float32).reshape(rows, HEADS, head)
    ).reshape(rows, width)
    keys = lax.all_gather(hist_keys, "seq", axis=1, tiled=True)
    values = lax.all_gather(hist_values, "seq", axis=1, tiled=True)
    hist_term = attend(q_part, keys[0], values[0], length)
    attn = hist_term + self_term
    gated = (layer_norm(attn) * u_part.astype(jnp.float32)).astype(jnp.bfloat16)
    projected = jnp.dot(
        gated, lax.all_gather(w_out, "grp", axis=0, tiled=True), preferred_element_type=jnp.float32
    )
    mixed = x32 + projected
    cand_index = (panel_map[:, None] * PANEL + jnp.arange(PANEL, dtype=jnp.int32)[None, :]).reshape(
        rows
    )
    valid = cand_index < cand_count[0]
    return jnp.where(valid[:, None], mixed, 0.0).astype(jnp.bfloat16)


def solution(mesh):
    return jax.shard_map(
        per_device,
        mesh=mesh,
        in_specs=(
            P(("grp", "seq"), None),
            P(),
            P("grp", None),
            P("grp", "seq", None),
            P("grp", "seq", None),
            P("grp"),
            P("grp"),
            P(("grp", "seq")),
        ),
        out_specs=P(("grp", "seq"), None),
        check_vma=False,
    )
```

profile of v0, /device:TPU:1, one launch (start us, length us, event | category | flops | bytes accessed | tf_op | source)
XLA Modules:
  0.0 220.0 jit_solution(5971789612150382788)
XLA Ops:
  6.5 0.0 all-gather.6.cloned.1.call-start
  6.5 0.7 all-gather.6.cloned.1.call-update
  7.3 0.0 all-gather.4.cloned.1.call-start
  7.3 2.0 copy.23
  9.3 0.0 all-gather.4.cloned.1.call-update
  9.4 0.0 all-gather.8.cloned.1.call-start
  9.4 0.7 all-gather.8.cloned.1.call-update
  10.1 1.2 convert_reduce_fusion
  11.3 1.3 fusion.7
  13.3 0.0 copy-start.2
  13.3 6.1 %multiply_convert_fusion = bf16[256,4096]{1,0:T(8,128)(2,1)S(1)} fusion(bf16[1024,4096]{1,0:T(8,128)(2,1)} %param.9, bf16[256,1024]{1,0:T(8,128)(2,1)} %param.8, f32[256]{0:T(256)S(1)} %add_sqrt_fusion.1, f32[256]{0:T(256)S(1)} %broadcast_multiply_fusion.1), kind=kOutput, calls=%fused_computation.3 | convolution fusion | flops 2153775104 | bytes 11012096 | tf_op jit(solution)/shard_map/dot_general | solution.py:44
  19.4 0.0 copy-start.1
  19.5 0.2 multiply_bitcast_fusion
  19.6 0.2 copy.33
  19.8 0.3 reduce_sum.47
  20.2 0.1 copy.28
  20.3 0.1 copy.29
  21.1 0.0 copy-done.2
  21.1 0.1 add_compare_fusion
  21.2 0.1 lt.25
  21.3 64.6 %all-gather.6.cloned.1.call-done = bf16[1,8192,1024]{2,1,0:T(8,128)(2,1)} async-done(((bf16[1,256,1024]{2,1,0:T(8,128)(2,1)}), bf16[1,8192,1024]{2,1,0:T(8,128)(2,1)}) %all-gather.6.cloned.1.call-update) | async-done | bytes 16777232 | tf_op jit(solution)/shard_map/all_gather | solution.py:59
  85.9 20.8 %copy.26 = bf16[1,8192,1024]{1,2,0:T(8,128)(2,1)} copy(bf16[1,8192,1024]{2,1,0:T(8,128)(2,1)} %all-gather.6.cloned.1.call-done) | data formatting | bytes 33554432 | tf_op jit(solution)/shard_map/all_gather | solution.py:59
  106.7 62.0 %all-gather.4.cloned.1.call-done = bf16[1,8192,1024]{1,2,0:T(8,128)(2,1)} async-done(((bf16[1,256,1024]{1,2,0:T(8,128)(2,1)}), bf16[1,8192,1024]{1,2,0:T(8,128)(2,1)}) %all-gather.4.cloned.1.call-update) | async-done | bytes 16777232 | tf_op jit(solution)/shard_map/all_gather | solution.py:58
  168.7 0.0 copy-done.1
  168.7 0.0 copy-start
  168.7 37.9 %fusion = f32[8,256,128]{1,2,0:T(8,128)} fusion(bf16[8192,8,128]{0,2,1:T(8,128)(2,1)} %bitcast.31, pred[8192]{0:T(1024)(128)(4,1)S(1)} %iota_compare_fusion, bf16[8192,8,128]{0,2,1:T(8,128)(2,1)} %bitcast.35, bf16[256,4096]{1,0:T(8,128)(2,1)S(1)} %multiply_convert_fusion), kind=kOutput, calls=%fused_computation.1 | convolution fusion | flops 8707375104 | bytes 35135488 | tf_op jit(solution)/shard_map/hrn,nhd->rhd/dot_general | solution.py:33
  206.6 1.6 copy.31
  208.2 0.3 mul.66
  208.5 1.4 fusion.27
  209.9 0.3 multiply_reduce_fusion
  210.1 0.0 all-gather.8.cloned.1.call-done
  210.2 0.0 copy-done
  210.2 3.3 %fusion.4 = bf16[256,1024]{1,0:T(8,128)(2,1)} fusion(bf16[1024,1024]{1,0:T(8,128)(2,1)} %all-gather.8.cloned.1.call-done, bf16[256,1024]{1,0:T(8,128)(2,1)S(1)} %copy-done, f32[256,1024]{1,0:T(8,128)S(1)} %get-tuple-element.6, bf16[256,4096]{1,0:T(8,128)(2,1)} %copy-done.1, f32[256]{0:T(256)S(1)} %add_sqrt_fusion, f32[256]{0:T(256)S(1)} %broadcast_multiply_fusion, ...), kind=kOutput, calls=%fused_computation.8 | convolution fusion | flops 539230208 | bytes 4720896 | tf_op jit(solution)/shard_map/dot_general | solution.py:63
  (7 shorter events, 0.1 us)
Async XLA Ops:
  6.5 79.3 %all-gather.6.cloned.1.call-start = ((), (), s32[]{:S(2)}) async-start(), calls=%async_computation.1 | async-start | bytes 17301504 | tf_op jit(solution)/shard_map/all_gather | solution.py:59
  7.3 161.4 %all-gather.4.cloned.1.call-start = ((), (), s32[]{:S(2)}) async-start(), calls=%async_computation | async-start | bytes 17301504 | tf_op jit(solution)/shard_map/all_gather | solution.py:58
  9.4 200.8 %all-gather.8.cloned.1.call-start = ((), (), s32[]{:S(2)}) async-start(), calls=%async_computation.2 | async-start | bytes 2621440 | tf_op jit(solution)/shard_map/all_gather | solution.py:64
  13.3 7.8 %copy-start.2 = (s32[8]{0:T(128)S(1)}, s32[8]{0:T(128)}, u32[]{:S(2)}) copy-start(s32[8]{0:T(128)} %param.15) | copy-start | bytes 100
  19.4 149.3 %copy-start.1 = (bf16[256,4096]{1,0:T(8,128)(2,1)}, bf16[256,4096]{1,0:T(8,128)(2,1)S(1)}, u32[]{:S(2)}) copy-start(bf16[256,4096]{1,0:T(8,128)(2,1)S(1)} %multiply_convert_fusion) | copy-start | bytes 6291460
  168.7 41.5 %copy-start = (bf16[256,1024]{1,0:T(8,128)(2,1)S(1)}, bf16[256,1024]{1,0:T(8,128)(2,1)}, u32[]{:S(2)}) copy-start(bf16[256,1024]{1,0:T(8,128)(2,1)} %param.8) | copy-start | bytes 1572868
Sparse Core Ops, SparseCore 0:
  9.6 76.2 all-gather.5
  88.1 80.5 all-gather.3
  170.4 30.4 all-gather.7
where the time goes:
time: 221 us; the launch traced here: 220 us
  waiting for transfers between devices  128 us (58%)
  matrix products  47.3 us (21%)
  local copies, waits for them, and re-layouts  25.2 us (11%)
  between operations  14.6 us (7%)
  other arithmetic  4.77 us (2%)
    all_gather x1, waiting for transfers between devices, per_device(): values = lax.all_gather(hist_values, 'seq', axis=1, tiled=True)  64.6 us
    all_gather x1, waiting for transfers between devices, per_device(): keys = lax.all_gather(hist_keys, 'seq', axis=1, tiled=True)  62 us
    dot_general x1, matrix products, attend(): jnp.einsum('hrn,nhd->rhd', weights, v_heads, preferred_element_type=jnp.f...  37.9 us
    all_gather x1, local copies, waits for them, and re-layouts, per_device(): values = lax.all_gather(hist_values, 'seq', axis=1, tiled=True)  20.8 us
    dot_general x1, matrix products, per_device(): jnp.dot(normed, w_in, preferred_element_type=jnp.float32)  6.11 us
  transfers between devices with their start and end apart: 3, of which 2 were waited for; matrix products, arithmetic and copies ran while one was open for 34% of the time, Pallas kernels for 0%

commit v1 on v0

v1 whole, which is shorter than its diff:
```python
import jax
import jax.numpy as jnp
from jax import lax
from jax.experimental import pallas as pl
from jax.experimental.pallas import tpu as pltpu
from jax.sharding import PartitionSpec as P

MESH = pl.DeviceIdType.MESH
HEADS = 8
PANEL = 32
ROWS = 256
D = 1024
HD = 128
eps = 1e-06
SCALE = HD**-0.5
NT = (((1,), (1,)), ((), ()))
BF = jnp.bfloat16
F32 = jnp.float32


def silu(z):
    h = z * 0.5
    return h + h * jnp.tanh(h)


def weight(s):
    h = (s * (0.5 * SCALE)).astype(BF)
    return h + h * jnp.tanh(h)


def layer_norm(x):
    mean = jnp.mean(x, axis=-1, keepdims=True)
    var = jnp.mean((x - mean) ** 2, axis=-1, keepdims=True)
    return (x - mean) / jnp.sqrt(var + eps)


def kernel(
    x_hbm,
    win_hbm,
    wout_hbm,
    hk_hbm,
    hv_hbm,
    hlen_ref,
    cnt_ref,
    pmap_ref,
    out_ref,
    x_v,
    n_v,
    win_v,
    hv_v,
    q_own,
    k_own,
    v_own,
    u_own,
    self_v,
    k_all,
    v_all,
    q_all,
    acc,
    osend,
    orecv,
    asend,
    attn_v,
    wout_v,
    loc,
    k_snd,
    k_rcv,
    v_snd,
    v_rcv,
    q_snd,
    q_rcv,
    o_snd,
    o_rcv,
    a_snd,
    a_rcv,
    w_snd,
    w_rcv,
):
    g = lax.axis_index("grp")
    s = lax.axis_index("seq")
    x, z, c = s // 8, (s // 2) % 4, s % 2
    xb, zb = x // 2, z // 2
    xh, zh = x + xb * (3 - 2 * x), z + zb * (3 - 2 * z)
    head = xh * 4 + zh * 2 + c

    def seq_of(x_, z_, c_):
        return x_ * 8 + z_ * 2 + c_

    def peer(d):
        d2, d1, d0 = d // 4, (d // 2) % 2, d % 2
        xp = xh + d2 * (1 - 2 * xh)
        zp = zh + d1 * (1 - 2 * zh)
        cp = c + d0 * (1 - 2 * c)
        return (g, seq_of(xp + xb * (3 - 2 * xp), zp + zb * (3 - 2 * zp), cp)), xp * 4 + zp * 2 + cp

    row_partner = (g, seq_of(x + (1 - c) * (3 - 2 * x), z + c * (3 - 2 * z), c))
    event_partner = (g, seq_of(x + c * (3 - 2 * x), z + (1 - c) * (3 - 2 * z), c))

    def cols(h):
        return pl.ds(pl.multiple_of(h * HD, HD), HD)

    def slot(d, n=1):
        return pl.ds(pl.multiple_of(d * ROWS, ROWS), n * ROWS)

    def remote(src, dst, snd, rcv, dev):
        return pltpu.make_async_remote_copy(
            src_ref=src, dst_ref=dst, send_sem=snd, recv_sem=rcv, device_id=dev, device_id_type=MESH
        )

    barrier = pltpu.get_barrier_semaphore()
    partners = [peer(d)[0] for d in range(1, 8)] + [row_partner, event_partner]
    partners += [((g + d) % 4, s) for d in range(1, 4)]
    for dev in partners:
        pl.semaphore_signal(barrier, inc=1, device_id=dev, device_id_type=MESH)

    ld_v = pltpu.make_async_copy(hv_hbm.at[0], hv_v, loc.at[0])
    ld_x = pltpu.make_async_copy(x_hbm, x_v, loc.at[1])
    ld_v.start()
    ld_x.start()
    ld_w = []
    for i, part in enumerate((2, 3, 1, 0)):
        cp = pltpu.make_async_copy(win_hbm.at[:, pl.ds(part * D, D)], win_v.at[part], loc.at[2 + i])
        cp.start()
        ld_w.append(cp)
    ld_wo = pltpu.make_async_copy(wout_hbm, wout_v.at[slot(g)], loc.at[6])
    ld_wo.start()
    own_k = pltpu.make_async_copy(hk_hbm.at[0, :, cols(head)], k_all.at[slot(0)], loc.at[7])
    own_k.start()

    ld_v.wait()
    pos = s * ROWS + lax.broadcasted_iota(jnp.int32, (ROWS, D), 0)
    hv_v[...] = jnp.where(pos < hlen_ref[0], hv_v[...].astype(F32), 0.0).astype(BF)

    pl.semaphore_wait(barrier, len(partners))

    sends = []

    def go(cp):
        cp.start()
        sends.append(cp)

    for d in range(1, 8):
        dev, h = peer(d)
        go(remote(hk_hbm.at[0, :, cols(h)], k_all.at[slot(d)], k_snd.at[d], k_rcv.at[d], dev))
    for d in range(1, 8):
        dev, h = peer(d)
        go(remote(hv_v.at[:, cols(h)], v_all.at[slot(d)], v_snd.at[d], v_rcv.at[d], dev))
    half = pl.ds(pl.multiple_of(c * 128, 128), 128)
    for d in range(1, 4):
        dst = wout_v.at[pl.ds(pl.multiple_of(g * 256 + c * 128, 128), 128)]
        go(remote(wout_hbm.at[half], dst, w_snd.at[d], w_rcv.at[d], ((g + d) % 4, s)))
    v_all[slot(0), :] = hv_v[:, cols(head)]

    ld_x.wait()
    n_v[...] = layer_norm(x_v[...].astype(F32)).astype(BF)

    def project(part, dst, lo, n):
        def piece(p, _):
            ds = pl.ds(pl.multiple_of(p * 256, 256), 256)
            dst[:, ds] = silu(jnp.dot(n_v[...], win_v[part, :, ds], preferred_element_type=F32)).astype(BF)
            return 0

        lax.fori_loop(lo, lo + n, piece, 0)

    ld_w[0].wait()
    project(2, q_own, 0, 4)
    for d in range(1, 8):
        dev, h = peer(d)
        go(remote(q_own.at[:, cols(h)], q_all.at[slot(d)], q_snd.at[d], q_rcv.at[d], dev))
    q_all[slot(0), :] = q_own[:, cols(head)]

    def arrived(buf, rcv, d):
        remote(buf.at[slot(d)], buf.at[slot(d)], rcv.at[d], rcv.at[d], event_partner).wait_recv()

    own_k.wait()
    work = [(3, k_own, i) for i in range(4)] + [(1, v_own, i) for i in range(4)] + [(0, u_own, i) for i in range(4)]
    done = 0
    for d in range(8):
        if d:
            arrived(k_all, k_rcv, d)
        go(remote(k_all.at[slot(d)], k_all.at[slot(8 + d)], k_snd.at[8 + d], k_rcv.at[8 + d], event_partner))
        if d:
            arrived(v_all, v_rcv, d)
        go(remote(v_all.at[slot(d)], v_all.at[slot(8 + d)], v_snd.at[8 + d], v_rcv.at[8 + d], event_partner))
        if d % 2 == 0:
            if d // 2 < 3:
                part, dst, _ = work[done]
                ld_w[1 + d // 2].wait()
                project(part, dst, 0, 4)
                done += 4
    for d in range(8):
        if d:
            arrived(q_all, q_rcv, d)
        go(remote(q_all.at[slot(d)], q_all.at[slot(8 + d)], q_snd.at[8 + d], q_rcv.at[8 + d], row_partner))

    for h in range(HEADS):
        ds = pl.ds(h * HD, HD)
        dot = jnp.sum(q_own[:, ds].astype(F32) * k_own[:, ds].astype(F32), axis=-1, keepdims=True)
        self_v[:, ds] = silu(dot * SCALE).astype(BF).astype(F32) * v_own[:, ds].astype(F32)

    def attend(rows, events):
        sc = lax.dot_general(q_all[rows, :], k_all[events, :], NT, preferred_element_type=F32)
        return jnp.dot(weight(sc), v_all[events, :], preferred_element_type=F32)

    def own_block(i, _):
        rows = slot(2 * i, 2)
        acc[rows, :] = attend(rows, pl.ds(0, 8 * ROWS))
        return 0

    lax.fori_loop(0, 4, own_block, 0)

    for d in range(1, 4):
        rows = pl.ds(pl.multiple_of(((g - d + 4) % 4) * 256 + c * 128, 128), 128)
        remote(wout_v.at[rows], wout_v.at[rows], w_rcv.at[d], w_rcv.at[d], event_partner).wait_recv()
        go(remote(wout_v.at[rows], wout_v.at[rows], w_snd.at[4 + d], w_rcv.at[4 + d], peer(1)[0]))

    for d in range(8, 16):
        arrived(k_all, k_rcv, d)
        arrived(v_all, v_rcv, d)
        arrived(q_all, q_rcv, d)

    def o_copy(i):
        return remote(osend.at[slot(2 * i, 2)], orecv.at[slot(2 * i, 2)], o_snd.at[i], o_rcv.at[i], row_partner)

    def partner_rows(n, _):
        i = 3 - n
        osend[slot(2 * i, 2), :] = attend(slot(8 + 2 * i, 2), pl.ds(0, 16 * ROWS)).astype(BF)
        o_copy(i).start()
        return 0

    lax.fori_loop(0, 4, partner_rows, 0)

    def a_copy(d):
        return remote(asend.at[slot(d)], attn_v.at[:, cols(head)], a_snd.at[d], a_rcv.at[d], peer(d)[0])

    def own_rows(n, _):
        i = 3 - n
        rows = slot(2 * i, 2)
        part = acc[rows, :] + attend(rows, pl.ds(8 * ROWS, 8 * ROWS))
        o_copy(i).wait_recv()
        asend[rows, :] = (part + orecv[rows, :].astype(F32)).astype(BF)
        a_copy(2 * i + 1).start()

        @pl.when(i > 0)
        def _():
            a_copy(2 * i).start()

        return 0

    lax.fori_loop(0, 4, own_rows, 0)
    attn_v[:, cols(head)] = asend[slot(0), :]

    for d in range(1, 4):
        rows = pl.ds(pl.multiple_of(((g - d + 4) % 4) * 256 + (1 - c) * 128, 128), 128)
        remote(wout_v.at[rows], wout_v.at[rows], w_rcv.at[4 + d], w_rcv.at[4 + d], event_partner).wait_recv()
    ld_wo.wait()
    for d in range(1, 8):
        h = peer(d)[1]
        remote(asend.at[slot(d)], attn_v.at[:, cols(h)], a_snd.at[d], a_rcv.at[d], event_partner).wait_recv()

    n_v[...] = (
        layer_norm(attn_v[...].astype(F32) + self_v[...]) * u_own[...].astype(F32)
    ).astype(BF)

    def out_piece(p, _):
        ds = pl.ds(pl.multiple_of(p * 256, 256), 256)
        mixed = x_v[:, ds].astype(F32) + jnp.dot(n_v[...], wout_v[:, ds], preferred_element_type=F32)
        for i in range(ROWS // PANEL):
            number = pmap_ref[i] * PANEL + lax.broadcasted_iota(jnp.int32, (PANEL, 256), 0)
            keep = mixed[i * PANEL : (i + 1) * PANEL]
            out_ref[pl.ds(i * PANEL, PANEL), ds] = jnp.where(number < cnt_ref[0], keep, 0.0).astype(BF)
        return 0

    lax.fori_loop(0, 4, out_piece, 0)

    for cp in sends:
        cp.wait_send()
    for i in range(4):
        o_copy(i).wait_send()
    for d in range(1, 8):
        a_copy(d).wait_send()


def per_device(cand_x, w_in, w_out, hist_keys, hist_values, hist_len, cand_count, panel_map):
    hbm = pl.BlockSpec(memory_space=pl.ANY)
    smem = pl.BlockSpec(memory_space=pltpu.SMEM)
    dma = pltpu.SemaphoreType.DMA
    return pl.pallas_call(
        kernel,
        out_shape=jax.ShapeDtypeStruct((ROWS, D), BF),
        in_specs=[hbm] * 5 + [smem] * 3,
        out_specs=pl.BlockSpec(memory_space=pltpu.VMEM),
        scratch_shapes=[
            pltpu.VMEM((ROWS, D), BF),
            pltpu.VMEM((ROWS, D), BF),
            pltpu.VMEM((4, D, D), BF),
            pltpu.VMEM((ROWS, D), BF),
            pltpu.VMEM((ROWS, D), BF),
            pltpu.VMEM((ROWS, D), BF),
            pltpu.VMEM((ROWS, D), BF),
            pltpu.VMEM((ROWS, D), BF),
            pltpu.VMEM((ROWS, D), F32),
            pltpu.VMEM((16 * ROWS, HD), BF),
            pltpu.VMEM((16 * ROWS, HD), BF),
            pltpu.VMEM((16 * ROWS, HD), BF),
            pltpu.VMEM((8 * ROWS, HD), F32),
            pltpu.VMEM((8 * ROWS, HD), BF),
            pltpu.VMEM((8 * ROWS, HD), BF),
            pltpu.VMEM((8 * ROWS, HD), BF),
            pltpu.VMEM((ROWS, D), BF),
            pltpu.VMEM((D, D), BF),
            dma((8,)),
            dma((16,)),
            dma((16,)),
            dma((16,)),
            dma((16,)),
            dma((16,)),
            dma((16,)),
            dma((4,)),
            dma((4,)),
            dma((8,)),
            dma((8,)),
            dma((8,)),
            dma((8,)),
        ],
        compiler_params=pltpu.CompilerParams(
            collective_id=0, has_side_effects=True, vmem_limit_bytes=56 * 2**20
        ),
    )(cand_x, w_in, w_out, hist_keys, hist_values, hist_len, cand_count, panel_map)


def solution(mesh):
    return jax.shard_map(
        per_device,
        mesh=mesh,
        in_specs=(
            P(("grp", "seq"), None),
            P(),
            P("grp", None),
            P("grp", "seq", None),
            P("grp", "seq", None),
            P("grp"),
            P("grp"),
            P(("grp", "seq")),
        ),
        out_specs=P(("grp", "seq"), None),
        check_vma=False,
    )
```

time: 221 us -> 61 us (0.28)
  waiting for transfers between devices: 128 us -> 0 us
  Pallas kernels: 0 us -> 57.6 us
  matrix products: 47.3 us -> 0 us
  local copies, waits for them, and re-layouts: 25.2 us -> 1.87 us
  between operations: 14.6 us -> 1.3 us
  other arithmetic: 4.77 us -> 0 us
    all_gather x3 -> x0, waiting for transfers between devices: 127 us -> none  [the longest x1 64.6 us: per_device(): values = lax.all_gather(hist_values, 'seq', axis=1, tiled=True)]
    pallas_call x0 -> x1, Pallas kernels: none -> 57.6 us  [per_device(): pl.pallas_call(kernel, out_shape=jax.ShapeDtypeStruct((ROWS, D), BF), in_...]
    dot_general x3 -> x0, matrix products: 47.3 us -> none  [the longest x1 37.9 us: attend(): jnp.einsum('hrn,nhd->rhd', weights, v_heads, preferred_element_type=jnp.f...]
    all_gather x1 -> x0, local copies, waits for them, and re-layouts: 20.8 us -> none  [per_device(): values = lax.all_gather(hist_values, 'seq', axis=1, tiled=True)]
    reduce_sum x5 -> x0, other arithmetic: 4.47 us -> none  [the longest x2 2.56 us: layer_norm(): mean = jnp.mean(x, axis=-1, keepdims=True)]
  transfers between devices with their start and end apart: 3 -> 0, of which waited for: 2 -> 0; matrix products, arithmetic and copies ran while one was open for 34% -> 0% of each run, Pallas kernels for 0% -> 0%
where the time goes in v1:
time: 61 us; the launch traced here: 60.8 us
  Pallas kernels  57.6 us (94%)
  local copies, waits for them, and re-layouts  1.87 us (3%)
  between operations  1.3 us (2%)
    pallas_call x1, Pallas kernels, per_device(): pl.pallas_call(kernel, out_shape=jax.ShapeDtypeStruct((ROWS, D), BF), in_...  57.6 us
    unnamed x1, local copies, waits for them, and re-layouts  1.87 us

profile of v1, /device:TPU:1, one launch (start us, length us, event | category | flops | bytes accessed | tf_op | source)
XLA Modules:
  0.0 60.8 jit_solution(8490162739162572740)
XLA Ops:
  1.3 57.6 %shard_map.82 = bf16[256,1024]{1,0:T(8,128)(2,1)} custom-call(bf16[256,1024]{1,0:T(8,128)(2,1)} %x_hbm.1, bf16[1024,4096]{1,0:T(8,128)(2,1)} %win_hbm.1, bf16[256,1024]{1,0:T(8,128)(2,1)} %wout_hbm.1, bf16[1,256,1024]{2,1,0:T(8,128)(2,1)} %hk_hbm.1, bf16[1,256,1024]{2,1,0:T(8,128)(2,1)} %hv_hbm.1, s32[1]{0:T(128)S(6)} %copy.10.hlen_ref, s32[1]{0:T(128)S(6)} %copy.11.cnt_ref, ...), custom_call_target="tpu_custom_call" | custom-call | tf_op jit(solution)/shard_map/pallas_call | solution.py:288
  58.9 1.9 %copy.12 = bf16[256,1024]{1,0:T(8,128)(2,1)} copy(bf16[256,1024]{1,0:T(8,128)(2,1)} %shard_map.82) | data formatting | bytes 1048576

commit v2 on v1

v2 whole, which is shorter than its diff:
```python
import jax
import jax.numpy as jnp
from jax import lax
from jax.experimental import pallas as pl
from jax.experimental.pallas import tpu as pltpu
from jax.sharding import PartitionSpec as P

MESH = pl.DeviceIdType.MESH
HEADS = 8
PANEL = 32
ROWS = 256
D = 1024
HD = 128
eps = 1e-06
SCALE = HD**-0.5
EVENT_AT = (0, 1, 2, 3, 4, 5, 12, 13, 6, 7, 8, 9, 10, 11, 14, 15)
ROW_AT = (4, 5, 0, 1, 2, 3, 12, 13, 6, 7, 8, 9, 10, 11, 14, 15)
NT = (((1,), (1,)), ((), ()))
BF = jnp.bfloat16
F32 = jnp.float32


def silu(z):
    h = z * 0.5
    return h + h * jnp.tanh(h)


def weight(s):
    h = (s * (0.5 * SCALE)).astype(BF)
    return h + h * jnp.tanh(h)


def layer_norm(x):
    mean = jnp.mean(x, axis=-1, keepdims=True)
    var = jnp.mean((x - mean) ** 2, axis=-1, keepdims=True)
    return (x - mean) / jnp.sqrt(var + eps)


def kernel(
    x_hbm,
    win_hbm,
    wout_hbm,
    hk_hbm,
    hv_hbm,
    hlen_hbm,
    cnt_hbm,
    pmap_hbm,
    out_ref,
    hlen_ref,
    cnt_ref,
    pmap_ref,
    x_v,
    n_v,
    win_v,
    hv_v,
    own_v,
    self_v,
    k_all,
    v_all,
    q_all,
    acc,
    osend,
    attn_v,
    wout_v,
    loc,
    k_snd,
    k_rcv,
    v_snd,
    v_rcv,
    q_snd,
    q_rcv,
    a_snd,
    a_rcv,
    w_snd,
    w_rcv,
):
    g = lax.axis_index("grp")
    s = lax.axis_index("seq")
    x, z, c = s // 8, (s // 2) % 4, s % 2
    xb, zb = x // 2, z // 2
    xh, zh = x + xb * (3 - 2 * x), z + zb * (3 - 2 * z)
    head = xh * 4 + zh * 2 + c

    def seq_of(x_, z_, c_):
        return x_ * 8 + z_ * 2 + c_

    def device(d, xb_, zb_):
        d2, d1, d0 = d // 4, (d // 2) % 2, d % 2
        xp = xh + d2 * (1 - 2 * xh)
        zp = zh + d1 * (1 - 2 * zh)
        cp = c + d0 * (1 - 2 * c)
        return (g, seq_of(xp + xb_ * (3 - 2 * xp), zp + zb_ * (3 - 2 * zp), cp)), xp * 4 + zp * 2 + cp

    def peer(d):
        return device(d, xb, zb)

    def across(d, core):
        return device(d, xb + (1 - core) * (1 - 2 * xb), zb + core * (1 - 2 * zb))

    row_partner = across(0, c)[0]
    event_partner = across(0, 1 - c)[0]

    def cols(h):
        return pl.ds(pl.multiple_of(h * HD, HD), HD)

    def block(i):
        return pl.ds(i * ROWS if isinstance(i, int) else pl.multiple_of(i * ROWS, ROWS), ROWS)

    def group(i):
        return pl.ds(i * 2 * ROWS if isinstance(i, int) else pl.multiple_of(i * 2 * ROWS, 2 * ROWS), 2 * ROWS)

    def ev(d):
        return block(EVENT_AT[d])

    def qs(d):
        return block(ROW_AT[d])

    def remote(src, dst, snd, rcv, dev):
        return pltpu.make_async_remote_copy(
            src_ref=src, dst_ref=dst, send_sem=snd, recv_sem=rcv, device_id=dev, device_id_type=MESH
        )

    barrier = pltpu.get_barrier_semaphore()
    senders = [peer(d)[0] for d in range(1, 8)] + [event_partner]
    for d in range(8):
        senders.append(across(d, (c + d % 2) % 2)[0])
    senders += [((g + d) % 4, s) for d in range(1, 4)]
    for dev in senders:
        pl.semaphore_signal(barrier, inc=1, device_id=dev, device_id_type=MESH)

    loads = [
        pltpu.make_async_copy(src, dst, loc.at[i])
        for i, (src, dst) in enumerate(
            [(x_hbm, x_v), (hlen_hbm, hlen_ref), (hv_hbm.at[0], hv_v)]
            + [(win_hbm.at[:, pl.ds(part * D, D)], win_v.at[part]) for part in (2, 3, 1, 0)]
            + [
                (wout_hbm, wout_v.at[block(g)]),
                (hk_hbm.at[0, :, cols(head)], k_all.at[ev(0)]),
                (cnt_hbm, cnt_ref),
                (pmap_hbm, pmap_ref),
            ]
        )
    ]
    for copy in loads:
        copy.start()

    def project(part, lo, n):
        ds = pl.ds(lo, n)
        own_v[part, :, ds] = silu(jnp.dot(n_v[...], win_v[part, :, ds], preferred_element_type=F32)).astype(BF)

    loads[0].wait()
    n_v[...] = layer_norm(x_v[...].astype(F32)).astype(BF)
    loads[1].wait()
    loads[2].wait()
    pos = s * ROWS + lax.broadcasted_iota(jnp.int32, (ROWS, D), 0)
    hv_v[...] = jnp.where(pos < hlen_ref[0], hv_v[...].astype(F32), 0.0).astype(BF)
    v_all[ev(0), :] = hv_v[:, cols(head)]
    loads[3].wait()
    project(2, 0, D)
    q_own = own_v.at[2]
    q_all[qs(0), :] = own_v[2, :, cols(head)]

    pl.semaphore_wait(barrier, len(senders))

    sends = []

    def go(copy):
        copy().start()
        sends.append(copy)

    def send_kv(d):
        dev, h = peer(d)
        go(lambda: remote(hk_hbm.at[0, :, cols(h)], k_all.at[ev(d)], k_snd.at[d], k_rcv.at[d], dev))
        go(lambda: remote(hv_v.at[:, cols(h)], v_all.at[ev(d)], v_snd.at[d], v_rcv.at[d], dev))

    def send_q(d):
        dev, h = peer(d)
        go(lambda: remote(q_own.at[:, cols(h)], q_all.at[qs(d)], q_snd.at[d], q_rcv.at[d], dev))

    def arrived(buf, rows, rcv, d):
        remote(buf.at[rows], buf.at[rows], rcv.at[d], rcv.at[d], event_partner).wait_recv()

    def await_kv(d):
        arrived(k_all, ev(d), k_rcv, d)
        arrived(v_all, ev(d), v_rcv, d)

    def await_q(d):
        arrived(q_all, qs(d), q_rcv, d)

    def pass_kv(d):
        if d:
            arrived(k_all, ev(d), k_rcv, d)
        k_src = k_all.at[ev(d)] if d else hk_hbm.at[0, :, cols(head)]
        go(lambda: remote(k_src, k_all.at[ev(8 + d)], k_snd.at[8 + d], k_rcv.at[8 + d], event_partner))
        if d:
            arrived(v_all, ev(d), v_rcv, d)
        go(lambda: remote(v_all.at[ev(d)], v_all.at[ev(8 + d)], v_snd.at[8 + d], v_rcv.at[8 + d], event_partner))

    def pass_q(d):
        if d:
            await_q(d)
        go(lambda: remote(q_all.at[qs(d)], q_all.at[qs(8 + d)], q_snd.at[8 + d], q_rcv.at[8 + d], row_partner))

    def w_rows(d, core):
        return pl.ds(pl.multiple_of(((g - d + 4) % 4) * 256 + core * 128, 128), 128)

    half = pl.ds(pl.multiple_of(c * 128, 128), 128)

    def send_w(d):
        dst = wout_v.at[w_rows(0, c)]
        go(lambda: remote(wout_hbm.at[half], dst, w_snd.at[d], w_rcv.at[d], ((g + d) % 4, s)))

    def pass_w(d):
        arrived(wout_v, w_rows(d, c), w_rcv, d)
        rows = wout_v.at[w_rows(d, c)]
        go(lambda: remote(rows, rows, w_snd.at[4 + d], w_rcv.at[4 + d], peer(1)[0]))

    send_kv(1)
    send_q(1)
    pass_kv(0)
    pass_q(0)
    for d in (2, 4, 3, 5):
        send_kv(d)
    for d in (2, 4, 3, 5):
        send_q(d)
    for d in (6, 7):
        send_kv(d)
    for d in (6, 7):
        send_q(d)
    for d in range(1, 4):
        send_w(d)

    for load in loads[4:7]:
        load.wait()
    pass_kv(1)
    pass_q(1)

    def rest(i, _):
        part = (2 - i) % 3 + (2 - i) // 2
        ds = pl.ds(0, D)
        own_v[part, :, ds] = silu(jnp.dot(n_v[...], win_v[part], preferred_element_type=F32)).astype(BF)
        return 0

    lax.fori_loop(0, 3, rest, 0)
    for h in range(HEADS):
        ds = pl.ds(h * HD, HD)
        dot = jnp.sum(own_v[2, :, ds].astype(F32) * own_v[3, :, ds].astype(F32), axis=-1, keepdims=True)
        self_v[:, ds] = silu(dot * SCALE).astype(BF).astype(F32) * own_v[1, :, ds].astype(F32)
    for d in (2, 4, 3, 5):
        pass_kv(d)

    def attend(rows, events):
        sc = lax.dot_general(q_all[rows, :], k_all[events, :], NT, preferred_element_type=F32)
        return jnp.dot(weight(sc), v_all[events, :], preferred_element_type=F32)

    loads[8].wait()

    def early(n, _):
        @pl.when(n == 1)
        def _():
            await_q(8)
            await_q(9)

        @pl.when(n == 2)
        def _():
            for d in (2, 4, 3, 5):
                pass_q(d)

        @pl.when(n == 4)
        def _():
            for d in range(8, 14):
                await_kv(d)

        @pl.when(n == 7)
        def _():
            pass_kv(6)

        @pl.when(n == 8)
        def _():
            for d in (10, 11, 12, 13):
                await_q(d)
            pass_kv(7)

        @pl.when(n == 10)
        def _():
            pass_q(6)
            pass_q(7)

        last = n // 8
        gr = (1 - last) * ((n + 2) % 4) + last * (n // 2)
        hf = (1 - last) * (n // 4) + last * (n % 2)
        events = pl.ds(pl.multiple_of(hf * 6 * ROWS, 6 * ROWS), 6 * ROWS)
        acc[hf, group(gr), :] = attend(group(gr), events)
        return 0

    lax.fori_loop(0, 12, early, 0)

    for d in range(1, 4):
        pass_w(d)

    def a_copy(d):
        if d < 8:
            dev = peer(d)[0]
        else:
            dev = across(d - 8, c)[0]
        return remote(osend.at[qs(d)], attn_v.at[d // 8, :, cols(head)], a_snd.at[d], a_rcv.at[d], dev)

    def send_sums(d):
        go(lambda: a_copy(d))

    for d in (14, 15):
        await_kv(d)
    late = pl.ds(12 * ROWS, 4 * ROWS)

    def finish(m, _):
        gr = (m + 3) % 6
        osend[group(gr), :] = (acc[0, group(gr), :] + acc[1, group(gr), :] + attend(group(gr), late)).astype(BF)
        for i, ds in enumerate(((8, 9), (10, 11), (12, 13), (2, 3), (4, 5), (1,))):

            @pl.when(m == i)
            def _():
                for d in ds:
                    send_sums(d)

        return 0

    lax.fori_loop(0, 6, finish, 0)
    attn_v[0, :, cols(head)] = osend[qs(0), :]

    def whole(m, _):
        @pl.when(m == 1)
        def _():
            await_q(14)
            await_q(15)

        osend[group(6 + m), :] = attend(group(6 + m), pl.ds(0, 16 * ROWS)).astype(BF)
        for i, ds in enumerate(((6, 7), (14, 15))):

            @pl.when(m == i)
            def _():
                for d in ds:
                    send_sums(d)

        return 0

    lax.fori_loop(0, 2, whole, 0)

    for d in range(1, 4):
        arrived(wout_v, w_rows(d, 1 - c), w_rcv, 4 + d)
    loads[7].wait()
    loads[9].wait()
    loads[10].wait()
    for d in range(1, 16):
        h = peer(d % 8)[1]
        remote(osend.at[qs(d)], attn_v.at[d // 8, :, cols(h)], a_snd.at[d], a_rcv.at[d], event_partner).wait_recv()

    attn = attn_v[0].astype(F32) + attn_v[1].astype(F32) + self_v[...]
    n_v[...] = (layer_norm(attn) * own_v[0].astype(F32)).astype(BF)

    def out_piece(p, _):
        ds = pl.ds(pl.multiple_of(p * 512, 512), 512)
        mixed = x_v[:, ds].astype(F32) + jnp.dot(n_v[...], wout_v[:, ds], preferred_element_type=F32)
        for i in range(ROWS // PANEL):
            number = pmap_ref[i] * PANEL + lax.broadcasted_iota(jnp.int32, (PANEL, 512), 0)
            keep = mixed[i * PANEL : (i + 1) * PANEL]
            out_ref[pl.ds(i * PANEL, PANEL), ds] = jnp.where(number < cnt_ref[0], keep, 0.0).astype(BF)
        return 0

    lax.fori_loop(0, 2, out_piece, 0)

    for copy in sends:
        copy().wait_send()


def per_device(cand_x, w_in, w_out, hist_keys, hist_values, hist_len, cand_count, panel_map):
    dma = pltpu.SemaphoreType.DMA
    return pl.pallas_call(
        kernel,
        out_shape=pltpu.VMEM((ROWS, D), BF),
        in_specs=[pl.BlockSpec(memory_space=pl.ANY)] * 8,
        out_specs=pl.BlockSpec(memory_space=pltpu.VMEM),
        scratch_shapes=[
            pltpu.SMEM((1,), jnp.int32),
            pltpu.SMEM((1,), jnp.int32),
            pltpu.SMEM((ROWS // PANEL,), jnp.int32),
            pltpu.VMEM((ROWS, D), BF),
            pltpu.VMEM((ROWS, D), BF),
            pltpu.VMEM((4, D, D), BF),
            pltpu.VMEM((ROWS, D), BF),
            pltpu.VMEM((4, ROWS, D), BF),
            pltpu.VMEM((ROWS, D), F32),
            pltpu.VMEM((16 * ROWS, HD), BF),
            pltpu.VMEM((16 * ROWS, HD), BF),
            pltpu.VMEM((16 * ROWS, HD), BF),
            pltpu.VMEM((2, 12 * ROWS, HD), F32),
            pltpu.VMEM((16 * ROWS, HD), BF),
            pltpu.VMEM((2, ROWS, D), BF),
            pltpu.VMEM((D, D), BF),
            dma((11,)),
            dma((16,)),
            dma((16,)),
            dma((16,)),
            dma((16,)),
            dma((16,)),
            dma((16,)),
            dma((16,)),
            dma((16,)),
            dma((8,)),
            dma((8,)),
        ],
        compiler_params=pltpu.CompilerParams(
            collective_id=0, has_side_effects=True, vmem_limit_bytes=48 * 2**20
        ),
    )(cand_x, w_in, w_out, hist_keys, hist_values, hist_len, cand_count, panel_map)


def solution(mesh):
    return jax.shard_map(
        per_device,
        mesh=mesh,
        in_specs=(
            P(("grp", "seq"), None),
            P(),
            P("grp", None),
            P("grp", "seq", None),
            P("grp", "seq", None),
            P("grp"),
            P("grp"),
            P(("grp", "seq")),
        ),
        out_specs=P(("grp", "seq"), None),
        check_vma=False,
    )
```

time: 61 us -> 56.7 us (0.930)
  Pallas kernels: 57.6 us -> 49.5 us
  local copies, waits for them, and re-layouts: 1.87 us -> 5.61 us
    pallas_call x1, Pallas kernels: 57.6 us -> 49.5 us  [per_device(): pl.pallas_call(kernel, out_shape=pltpu.VMEM((ROWS, D), BF), in_specs=[pl....]
    unnamed x1 -> x11, local copies, waits for them, and re-layouts: 1.87 us -> 5.61 us
where the time goes in v2:
time: 56.7 us; the launch traced here: 56.4 us
  Pallas kernels  49.5 us (87%)
  local copies, waits for them, and re-layouts  5.61 us (10%)
  between operations  1.32 us (2%)
    pallas_call x1, Pallas kernels, per_device(): pl.pallas_call(kernel, out_shape=pltpu.VMEM((ROWS, D), BF), in_specs=[pl....  49.5 us
    unnamed x11, local copies, waits for them, and re-layouts  5.61 us

profile of v2, /device:TPU:1, one launch (start us, length us, event | category | flops | bytes accessed | tf_op | source)
XLA Modules:
  0.0 56.4 jit_solution(10859819631862880768)
XLA Ops:
  1.3 0.0 copy-start
  1.3 1.0 %copy-done = bf16[256,1024]{1,0:T(8,128)(2,1)S(1)} copy-done((bf16[256,1024]{1,0:T(8,128)(2,1)S(1)}, bf16[256,1024]{1,0:T(8,128)(2,1)}, u32[]{:S(2)}) %copy-start) | copy-done | bytes 524312
  2.3 0.0 copy-start.1
  2.3 1.0 %copy-done.1 = bf16[256,1024]{1,0:T(8,128)(2,1)S(1)} copy-done((bf16[256,1024]{1,0:T(8,128)(2,1)S(1)}, bf16[256,1024]{1,0:T(8,128)(2,1)}, u32[]{:S(2)}) %copy-start.1) | copy-done | bytes 524312
  3.4 0.0 copy-start.2
  3.4 1.0 %copy-done.2 = bf16[1,256,1024]{2,1,0:T(8,128)(2,1)S(1)} copy-done((bf16[1,256,1024]{2,1,0:T(8,128)(2,1)S(1)}, bf16[1,256,1024]{2,1,0:T(8,128)(2,1)}, u32[]{:S(2)}) %copy-start.2) | copy-done | bytes 524312
  4.4 0.0 copy-start.3
  4.4 1.0 %copy-done.3 = bf16[1,256,1024]{2,1,0:T(8,128)(2,1)S(1)} copy-done((bf16[1,256,1024]{2,1,0:T(8,128)(2,1)S(1)}, bf16[1,256,1024]{2,1,0:T(8,128)(2,1)}, u32[]{:S(2)}) %copy-start.3) | copy-done | bytes 524312
  5.5 0.0 copy-start.4
  5.5 0.7 %copy-done.4 = s32[8]{0:T(128)S(1)} copy-done((s32[8]{0:T(128)S(1)}, s32[8]{0:T(128)}, u32[]{:S(2)}) %copy-start.4) | copy-done | bytes 56
  6.1 49.5 %shard_map.82 = bf16[256,1024]{1,0:T(8,128)(2,1)S(1)} custom-call(bf16[256,1024]{1,0:T(8,128)(2,1)S(1)} %copy-done, bf16[1024,4096]{1,0:T(8,128)(2,1)} %win_hbm.1, bf16[256,1024]{1,0:T(8,128)(2,1)S(1)} %copy-done.1, bf16[1,256,1024]{2,1,0:T(8,128)(2,1)S(1)} %copy-done.2, bf16[1,256,1024]{2,1,0:T(8,128)(2,1)S(1)} %copy-done.3, s32[1]{0:T(128)S(6)} %copy.11.hlen_hbm, ...), custom_call_target="tpu_custom_call" | custom-call | tf_op jit(solution)/shard_map/pallas_call | solution.py:377
  55.6 0.8 %copy.10 = bf16[256,1024]{1,0:T(8,128)(2,1)} copy(bf16[256,1024]{1,0:T(8,128)(2,1)S(1)} %shard_map.82) | data formatting | bytes 1048576
Async XLA Ops:
  1.3 1.0 %copy-start = (bf16[256,1024]{1,0:T(8,128)(2,1)S(1)}, bf16[256,1024]{1,0:T(8,128)(2,1)}, u32[]{:S(2)}) copy-start(bf16[256,1024]{1,0:T(8,128)(2,1)} %x_hbm.1) | copy-start | bytes 1572868
  2.3 1.0 %copy-start.1 = (bf16[256,1024]{1,0:T(8,128)(2,1)S(1)}, bf16[256,1024]{1,0:T(8,128)(2,1)}, u32[]{:S(2)}) copy-start(bf16[256,1024]{1,0:T(8,128)(2,1)} %wout_hbm.1) | copy-start | bytes 1572868
  3.4 1.0 %copy-start.2 = (bf16[1,256,1024]{2,1,0:T(8,128)(2,1)S(1)}, bf16[1,256,1024]{2,1,0:T(8,128)(2,1)}, u32[]{:S(2)}) copy-start(bf16[1,256,1024]{2,1,0:T(8,128)(2,1)} %hk_hbm.1) | copy-start | bytes 1572868
  4.4 1.0 %copy-start.3 = (bf16[1,256,1024]{2,1,0:T(8,128)(2,1)S(1)}, bf16[1,256,1024]{2,1,0:T(8,128)(2,1)}, u32[]{:S(2)}) copy-start(bf16[1,256,1024]{2,1,0:T(8,128)(2,1)} %hv_hbm.1) | copy-start | bytes 1572868
  5.5 0.7 %copy-start.4 = (s32[8]{0:T(128)S(1)}, s32[8]{0:T(128)}, u32[]{:S(2)}) copy-start(s32[8]{0:T(128)} %pmap_hbm.1) | copy-start | bytes 100

commit v3 on v2

--- a/solution.py
+++ b/solution.py
@@ -121,11 +121,9 @@
         )
 
     barrier = pltpu.get_barrier_semaphore()
-    senders = [peer(d)[0] for d in range(1, 8)] + [event_partner]
-    for d in range(8):
-        senders.append(across(d, (c + d % 2) % 2)[0])
-    senders += [((g + d) % 4, s) for d in range(1, 4)]
-    for dev in senders:
+    partners = [peer(d)[0] for d in range(1, 8)] + [row_partner, event_partner]
+    partners += [((g + d) % 4, s) for d in range(1, 4)]
+    for dev in partners:
         pl.semaphore_signal(barrier, inc=1, device_id=dev, device_id_type=MESH)
 
     loads = [
@@ -141,26 +139,23 @@
             ]
         )
     ]
-    for copy in loads:
-        copy.start()
-
-    def project(part, lo, n):
-        ds = pl.ds(lo, n)
-        own_v[part, :, ds] = silu(jnp.dot(n_v[...], win_v[part, :, ds], preferred_element_type=F32)).astype(BF)
-
-    loads[0].wait()
-    n_v[...] = layer_norm(x_v[...].astype(F32)).astype(BF)
+    for i in (1, 2, 0, 3):
+        loads[i].start()
+
     loads[1].wait()
     loads[2].wait()
     pos = s * ROWS + lax.broadcasted_iota(jnp.int32, (ROWS, D), 0)
     hv_v[...] = jnp.where(pos < hlen_ref[0], hv_v[...].astype(F32), 0.0).astype(BF)
     v_all[ev(0), :] = hv_v[:, cols(head)]
+    loads[0].wait()
+    n_v[...] = layer_norm(x_v[...].astype(F32)).astype(BF)
+    for i in (4, 5, 6, 7, 8, 9, 10):
+        loads[i].start()
     loads[3].wait()
-    project(2, 0, D)
-    q_own = own_v.at[2]
+    own_v[2] = silu(jnp.dot(n_v[...], win_v[2], preferred_element_type=F32)).astype(BF)
     q_all[qs(0), :] = own_v[2, :, cols(head)]
 
-    pl.semaphore_wait(barrier, len(senders))
+    pl.semaphore_wait(barrier, len(partners))
 
     sends = []
 
@@ -168,10 +163,15 @@
         copy().start()
         sends.append(copy)
 
-    def send_kv(d):
+    def send_k(d):
         dev, h = peer(d)
         go(lambda: remote(hk_hbm.at[0, :, cols(h)], k_all.at[ev(d)], k_snd.at[d], k_rcv.at[d], dev))
+
+    def send_v(d):
+        dev, h = peer(d)
         go(lambda: remote(hv_v.at[:, cols(h)], v_all.at[ev(d)], v_snd.at[d], v_rcv.at[d], dev))
+
+    q_own = own_v.at[2]
 
     def send_q(d):
         dev, h = peer(d)
@@ -187,14 +187,20 @@
     def await_q(d):
         arrived(q_all, qs(d), q_rcv, d)
 
-    def pass_kv(d):
+    def pass_k(d):
         if d:
             arrived(k_all, ev(d), k_rcv, d)
         k_src = k_all.at[ev(d)] if d else hk_hbm.at[0, :, cols(head)]
         go(lambda: remote(k_src, k_all.at[ev(8 + d)], k_snd.at[8 + d], k_rcv.at[8 + d], event_partner))
+
+    def pass_v(d):
         if d:
             arrived(v_all, ev(d), v_rcv, d)
         go(lambda: remote(v_all.at[ev(d)], v_all.at[ev(8 + d)], v_snd.at[8 + d], v_rcv.at[8 + d], event_partner))
+
+    def pass_kv(d):
+        pass_k(d)
+        pass_v(d)
 
     def pass_q(d):
         if d:
@@ -215,25 +221,35 @@
         rows = wout_v.at[w_rows(d, c)]
         go(lambda: remote(rows, rows, w_snd.at[4 + d], w_rcv.at[4 + d], peer(1)[0]))
 
-    send_kv(1)
+    near = (2, 4, 3, 5)
+    for d in near:
+        send_k(d)
+    send_k(1)
+    pass_k(0)
+
+    for d in near:
+        send_v(d)
+    send_v(1)
+    pass_v(0)
+
+    for d in near:
+        send_q(d)
     send_q(1)
-    pass_kv(0)
     pass_q(0)
-    for d in (2, 4, 3, 5):
-        send_kv(d)
-    for d in (2, 4, 3, 5):
-        send_q(d)
     for d in (6, 7):
-        send_kv(d)
+        send_k(d)
+        send_v(d)
     for d in (6, 7):
         send_q(d)
     for d in range(1, 4):
         send_w(d)
 
+    pass_kv(1)
+    pass_q(1)
+    for d in near:
+        pass_k(d)
     for load in loads[4:7]:
         load.wait()
-    pass_kv(1)
-    pass_q(1)
 
     def rest(i, _):
         part = (2 - i) % 3 + (2 - i) // 2
@@ -246,8 +262,8 @@
         ds = pl.ds(h * HD, HD)
         dot = jnp.sum(own_v[2, :, ds].astype(F32) * own_v[3, :, ds].astype(F32), axis=-1, keepdims=True)
         self_v[:, ds] = silu(dot * SCALE).astype(BF).astype(F32) * own_v[1, :, ds].astype(F32)
-    for d in (2, 4, 3, 5):
-        pass_kv(d)
+    for d in near:
+        pass_v(d)
 
     def attend(rows, events):
         sc = lax.dot_general(q_all[rows, :], k_all[events, :], NT, preferred_element_type=F32)
@@ -263,7 +279,7 @@
 
         @pl.when(n == 2)
         def _():
-            for d in (2, 4, 3, 5):
+            for d in near:
                 pass_q(d)
 
         @pl.when(n == 4)
@@ -273,27 +289,27 @@
 
         @pl.when(n == 7)
         def _():
-            pass_kv(6)
-
-        @pl.when(n == 8)
-        def _():
             for d in (10, 11, 12, 13):
                 await_q(d)
+            pass_kv(6)
+
+        @pl.when(n == 8)
+        def _():
             pass_kv(7)
 
-        @pl.when(n == 10)
+        @pl.when(n == 9)
         def _():
             pass_q(6)
             pass_q(7)
 
-        last = n // 8
-        gr = (1 - last) * ((n + 2) % 4) + last * (n // 2)
-        hf = (1 - last) * (n // 4) + last * (n % 2)
+        last = (n + 1) // 8
+        gr = (1 - last) * ((n + 2 - 3 * (n // 4)) % 4) + last * ((n + 1) // 2)
+        hf = (1 - last) * (n // 4) + last * ((n + 1) % 2)
         events = pl.ds(pl.multiple_of(hf * 6 * ROWS, 6 * ROWS), 6 * ROWS)
         acc[hf, group(gr), :] = attend(group(gr), events)
         return 0
 
-    lax.fori_loop(0, 12, early, 0)
+    lax.fori_loop(0, 11, early, 0)
 
     for d in range(1, 4):
         pass_w(d)
@@ -315,7 +331,7 @@
     def finish(m, _):
         gr = (m + 3) % 6
         osend[group(gr), :] = (acc[0, group(gr), :] + acc[1, group(gr), :] + attend(group(gr), late)).astype(BF)
-        for i, ds in enumerate(((8, 9), (10, 11), (12, 13), (2, 3), (4, 5), (1,))):
+        for i, ds in enumerate(((8, 9), (10, 11), (12, 13), (2, 3), (4, 5))):
 
             @pl.when(m == i)
             def _():
@@ -324,17 +340,11 @@
 
         return 0
 
-    lax.fori_loop(0, 6, finish, 0)
-    attn_v[0, :, cols(head)] = osend[qs(0), :]
+    lax.fori_loop(0, 5, finish, 0)
 
     def whole(m, _):
-        @pl.when(m == 1)
-        def _():
-            await_q(14)
-            await_q(15)
-
-        osend[group(6 + m), :] = attend(group(6 + m), pl.ds(0, 16 * ROWS)).astype(BF)
-        for i, ds in enumerate(((6, 7), (14, 15))):
+        osend[group(7 - m), :] = attend(group(7 - m), pl.ds(0, 16 * ROWS)).astype(BF)
+        for i, ds in enumerate(((14, 15), (6, 7))):
 
             @pl.when(m == i)
             def _():
@@ -343,7 +353,13 @@
 
         return 0
 
+    await_q(14)
+    await_q(15)
     lax.fori_loop(0, 2, whole, 0)
+
+    osend[group(2), :] = (acc[0, group(2), :] + attend(group(2), pl.ds(6 * ROWS, 10 * ROWS))).astype(BF)
+    send_sums(1)
+    attn_v[0, :, cols(head)] = osend[qs(0), :]
 
     for d in range(1, 4):
         arrived(wout_v, w_rows(d, 1 - c), w_rcv, 4 + d)
@@ -377,7 +393,7 @@
     return pl.pallas_call(
         kernel,
         out_shape=pltpu.VMEM((ROWS, D), BF),
-        in_specs=[pl.BlockSpec(memory_space=pl.ANY)] * 8,
+        in_specs=[pl.BlockSpec(memory_space=pltpu.HBM)] * 8,
         out_specs=pl.BlockSpec(memory_space=pltpu.VMEM),
         scratch_shapes=[
             pltpu.SMEM((1,), jnp.int32),
@@ -409,7 +425,7 @@
             dma((8,)),
         ],
         compiler_params=pltpu.CompilerParams(
-            collective_id=0, has_side_effects=True, vmem_limit_bytes=48 * 2**20
+            collective_id=0, has_side_effects=True, vmem_limit_bytes=56 * 2**20
         ),
     )(cand_x, w_in, w_out, hist_keys, hist_values, hist_len, cand_count, panel_map)
 

time: 56.7 us -> 50.2 us (0.89)
  local copies, waits for them, and re-layouts: 5.61 us -> 0.8 us
  Pallas kernels: 49.5 us -> 48 us
    unnamed x11 -> x1, local copies, waits for them, and re-layouts: 5.61 us -> 0.8 us
    pallas_call x1, Pallas kernels: 49.5 us -> 48 us  [per_device(): pl.pallas_call(kernel, out_shape=pltpu.VMEM((ROWS, D), BF), in_specs=[pl....]
where the time goes in v3:
time: 50.2 us; the launch traced here: 50.1 us
  Pallas kernels  48 us (96%)
  between operations  1.3 us (3%)
  local copies, waits for them, and re-layouts  0.8 us (2%)
    pallas_call x1, Pallas kernels, per_device(): pl.pallas_call(kernel, out_shape=pltpu.VMEM((ROWS, D), BF), in_specs=[pl....  48 us

profile of v3, /device:TPU:1, one launch (start us, length us, event | category | flops | bytes accessed | tf_op | source)
XLA Modules:
  0.0 50.1 jit_solution(2908336238130601073)
XLA Ops:
  1.3 48.0 %shard_map.82 = bf16[256,1024]{1,0:T(8,128)(2,1)S(1)} custom-call(bf16[256,1024]{1,0:T(8,128)(2,1)} %x_hbm.1, bf16[1024,4096]{1,0:T(8,128)(2,1)} %win_hbm.1, bf16[256,1024]{1,0:T(8,128)(2,1)} %wout_hbm.1, bf16[1,256,1024]{2,1,0:T(8,128)(2,1)} %hk_hbm.1, bf16[1,256,1024]{2,1,0:T(8,128)(2,1)} %hv_hbm.1, s32[1]{0:T(128)S(6)} %copy.11.hlen_hbm, ...), custom_call_target="tpu_custom_call" | custom-call | tf_op jit(solution)/shard_map/pallas_call | solution.py:393
  49.3 0.8 %copy.10 = bf16[256,1024]{1,0:T(8,128)(2,1)} copy(bf16[256,1024]{1,0:T(8,128)(2,1)S(1)} %shard_map.82) | data formatting | bytes 1048576

commit v4 on v3

--- a/solution.py
+++ b/solution.py
@@ -149,89 +149,88 @@
     v_all[ev(0), :] = hv_v[:, cols(head)]
     loads[0].wait()
     n_v[...] = layer_norm(x_v[...].astype(F32)).astype(BF)
+    pl.semaphore_wait(barrier, len(partners))
+
+    sends = []
+
+    def go(copy):
+        copy().start()
+        sends.append(copy)
+
+    def send_k(d):
+        dev, h = peer(d)
+        go(lambda: remote(hk_hbm.at[0, :, cols(h)], k_all.at[ev(d)], k_snd.at[d], k_rcv.at[d], dev))
+
+    def send_v(d):
+        dev, h = peer(d)
+        go(lambda: remote(hv_v.at[:, cols(h)], v_all.at[ev(d)], v_snd.at[d], v_rcv.at[d], dev))
+
+    q_own = own_v.at[2]
+
+    def send_q(d):
+        dev, h = peer(d)
+        go(lambda: remote(q_own.at[:, cols(h)], q_all.at[qs(d)], q_snd.at[d], q_rcv.at[d], dev))
+
+    def arrived(buf, rows, rcv, d):
+        remote(buf.at[rows], buf.at[rows], rcv.at[d], rcv.at[d], event_partner).wait_recv()
+
+    def await_kv(d):
+        arrived(k_all, ev(d), k_rcv, d)
+        arrived(v_all, ev(d), v_rcv, d)
+
+    def await_q(d):
+        arrived(q_all, qs(d), q_rcv, d)
+
+    def pass_k(d):
+        if d:
+            arrived(k_all, ev(d), k_rcv, d)
+        k_src = k_all.at[ev(d)] if d else hk_hbm.at[0, :, cols(head)]
+        go(lambda: remote(k_src, k_all.at[ev(8 + d)], k_snd.at[8 + d], k_rcv.at[8 + d], event_partner))
+
+    def pass_v(d):
+        if d:
+            arrived(v_all, ev(d), v_rcv, d)
+        go(lambda: remote(v_all.at[ev(d)], v_all.at[ev(8 + d)], v_snd.at[8 + d], v_rcv.at[8 + d], event_partner))
+
+    def pass_kv(d):
+        pass_k(d)
+        pass_v(d)
+
+    def pass_q(d):
+        if d:
+            await_q(d)
+        go(lambda: remote(q_all.at[qs(d)], q_all.at[qs(8 + d)], q_snd.at[8 + d], q_rcv.at[8 + d], row_partner))
+
+    def w_rows(d, core):
+        return pl.ds(pl.multiple_of(((g - d + 4) % 4) * 256 + core * 128, 128), 128)
+
+    half = pl.ds(pl.multiple_of(c * 128, 128), 128)
+
+    def send_w(d):
+        dst = wout_v.at[w_rows(0, c)]
+        go(lambda: remote(wout_hbm.at[half], dst, w_snd.at[d], w_rcv.at[d], ((g + d) % 4, s)))
+
+    def pass_w(d):
+        arrived(wout_v, w_rows(d, c), w_rcv, d)
+        rows = wout_v.at[w_rows(d, c)]
+        go(lambda: remote(rows, rows, w_snd.at[4 + d], w_rcv.at[4 + d], peer(1)[0]))
+
+    near = (2, 4, 3, 5)
+    for d in near:
+        send_k(d)
+    send_k(1)
+    pass_k(0)
+
+    for d in near:
+        send_v(d)
+    send_v(1)
+    pass_v(0)
+
     for i in (4, 5, 6, 7, 8, 9, 10):
         loads[i].start()
     loads[3].wait()
     own_v[2] = silu(jnp.dot(n_v[...], win_v[2], preferred_element_type=F32)).astype(BF)
     q_all[qs(0), :] = own_v[2, :, cols(head)]
-
-    pl.semaphore_wait(barrier, len(partners))
-
-    sends = []
-
-    def go(copy):
-        copy().start()
-        sends.append(copy)
-
-    def send_k(d):
-        dev, h = peer(d)
-        go(lambda: remote(hk_hbm.at[0, :, cols(h)], k_all.at[ev(d)], k_snd.at[d], k_rcv.at[d], dev))
-
-    def send_v(d):
-        dev, h = peer(d)
-        go(lambda: remote(hv_v.at[:, cols(h)], v_all.at[ev(d)], v_snd.at[d], v_rcv.at[d], dev))
-
-    q_own = own_v.at[2]
-
-    def send_q(d):
-        dev, h = peer(d)
-        go(lambda: remote(q_own.at[:, cols(h)], q_all.at[qs(d)], q_snd.at[d], q_rcv.at[d], dev))
-
-    def arrived(buf, rows, rcv, d):
-        remote(buf.at[rows], buf.at[rows], rcv.at[d], rcv.at[d], event_partner).wait_recv()
-
-    def await_kv(d):
-        arrived(k_all, ev(d), k_rcv, d)
-        arrived(v_all, ev(d), v_rcv, d)
-
-    def await_q(d):
-        arrived(q_all, qs(d), q_rcv, d)
-
-    def pass_k(d):
-        if d:
-            arrived(k_all, ev(d), k_rcv, d)
-        k_src = k_all.at[ev(d)] if d else hk_hbm.at[0, :, cols(head)]
-        go(lambda: remote(k_src, k_all.at[ev(8 + d)], k_snd.at[8 + d], k_rcv.at[8 + d], event_partner))
-
-    def pass_v(d):
-        if d:
-            arrived(v_all, ev(d), v_rcv, d)
-        go(lambda: remote(v_all.at[ev(d)], v_all.at[ev(8 + d)], v_snd.at[8 + d], v_rcv.at[8 + d], event_partner))
-
-    def pass_kv(d):
-        pass_k(d)
-        pass_v(d)
-
-    def pass_q(d):
-        if d:
-            await_q(d)
-        go(lambda: remote(q_all.at[qs(d)], q_all.at[qs(8 + d)], q_snd.at[8 + d], q_rcv.at[8 + d], row_partner))
-
-    def w_rows(d, core):
-        return pl.ds(pl.multiple_of(((g - d + 4) % 4) * 256 + core * 128, 128), 128)
-
-    half = pl.ds(pl.multiple_of(c * 128, 128), 128)
-
-    def send_w(d):
-        dst = wout_v.at[w_rows(0, c)]
-        go(lambda: remote(wout_hbm.at[half], dst, w_snd.at[d], w_rcv.at[d], ((g + d) % 4, s)))
-
-    def pass_w(d):
-        arrived(wout_v, w_rows(d, c), w_rcv, d)
-        rows = wout_v.at[w_rows(d, c)]
-        go(lambda: remote(rows, rows, w_snd.at[4 + d], w_rcv.at[4 + d], peer(1)[0]))
-
-    near = (2, 4, 3, 5)
-    for d in near:
-        send_k(d)
-    send_k(1)
-    pass_k(0)
-
-    for d in near:
-        send_v(d)
-    send_v(1)
-    pass_v(0)
-
     for d in near:
         send_q(d)
     send_q(1)
@@ -287,29 +286,31 @@
             for d in range(8, 14):
                 await_kv(d)
 
+        @pl.when(n == 5)
+        def _():
+            pass_kv(6)
+            pass_kv(7)
+
+        @pl.when(n == 6)
+        def _():
+            await_q(10)
+            await_q(11)
+
         @pl.when(n == 7)
-        def _():
-            for d in (10, 11, 12, 13):
-                await_q(d)
-            pass_kv(6)
-
-        @pl.when(n == 8)
-        def _():
-            pass_kv(7)
-
-        @pl.when(n == 9)
         def _():
             pass_q(6)
             pass_q(7)
-
-        last = (n + 1) // 8
-        gr = (1 - last) * ((n + 2 - 3 * (n // 4)) % 4) + last * ((n + 1) // 2)
-        hf = (1 - last) * (n // 4) + last * ((n + 1) % 2)
+            await_q(12)
+            await_q(13)
+
+        last = n // 6
+        gr = (1 - last) * ((n + 2 - 2 * (n // 4)) % 4) + last * (1 + n // 2)
+        hf = (1 - last) * (n // 4) + last * (n % 2)
         events = pl.ds(pl.multiple_of(hf * 6 * ROWS, 6 * ROWS), 6 * ROWS)
         acc[hf, group(gr), :] = attend(group(gr), events)
         return 0
 
-    lax.fori_loop(0, 11, early, 0)
+    lax.fori_loop(0, 10, early, 0)
 
     for d in range(1, 4):
         pass_w(d)
@@ -329,9 +330,9 @@
     late = pl.ds(12 * ROWS, 4 * ROWS)
 
     def finish(m, _):
-        gr = (m + 3) % 6
+        gr = (m + 4) % 6
         osend[group(gr), :] = (acc[0, group(gr), :] + acc[1, group(gr), :] + attend(group(gr), late)).astype(BF)
-        for i, ds in enumerate(((8, 9), (10, 11), (12, 13), (2, 3), (4, 5))):
+        for i, ds in enumerate(((10, 11), (12, 13), (2, 3), (4, 5))):
 
             @pl.when(m == i)
             def _():
@@ -340,7 +341,7 @@
 
         return 0
 
-    lax.fori_loop(0, 5, finish, 0)
+    lax.fori_loop(0, 4, finish, 0)
 
     def whole(m, _):
         osend[group(7 - m), :] = attend(group(7 - m), pl.ds(0, 16 * ROWS)).astype(BF)
@@ -357,8 +358,19 @@
     await_q(15)
     lax.fori_loop(0, 2, whole, 0)
 
-    osend[group(2), :] = (acc[0, group(2), :] + attend(group(2), pl.ds(6 * ROWS, 10 * ROWS))).astype(BF)
-    send_sums(1)
+    def near_rows(m, _):
+        gr = 3 - m
+        osend[group(gr), :] = (acc[0, group(gr), :] + attend(group(gr), pl.ds(6 * ROWS, 10 * ROWS))).astype(BF)
+        for i, ds in enumerate(((8, 9), (1,))):
+
+            @pl.when(m == i)
+            def _():
+                for d in ds:
+                    send_sums(d)
+
+        return 0
+
+    lax.fori_loop(0, 2, near_rows, 0)
     attn_v[0, :, cols(head)] = osend[qs(0), :]
 
     for d in range(1, 4):

time: 50.2 us -> 48.6 us (0.968)
  Pallas kernels: 48 us -> 46.1 us
    pallas_call x1, Pallas kernels: 48 us -> 46.1 us  [per_device(): pl.pallas_call(kernel, out_shape=pltpu.VMEM((ROWS, D), BF), in_specs=[pl....]
where the time goes in v4:
time: 48.6 us; the launch traced here: 48.2 us
  Pallas kernels  46.1 us (95%)
  between operations  1.3 us (3%)
  local copies, waits for them, and re-layouts  0.8 us (2%)
    pallas_call x1, Pallas kernels, per_device(): pl.pallas_call(kernel, out_shape=pltpu.VMEM((ROWS, D), BF), in_specs=[pl....  46.1 us

profile of v4, /device:TPU:1, one launch (start us, length us, event | category | flops | bytes accessed | tf_op | source)
XLA Modules:
  0.0 48.2 jit_solution(3794671330180431121)
XLA Ops:
  1.3 46.1 %shard_map.82 = bf16[256,1024]{1,0:T(8,128)(2,1)S(1)} custom-call(bf16[256,1024]{1,0:T(8,128)(2,1)} %x_hbm.1, bf16[1024,4096]{1,0:T(8,128)(2,1)} %win_hbm.1, bf16[256,1024]{1,0:T(8,128)(2,1)} %wout_hbm.1, bf16[1,256,1024]{2,1,0:T(8,128)(2,1)} %hk_hbm.1, bf16[1,256,1024]{2,1,0:T(8,128)(2,1)} %hv_hbm.1, s32[1]{0:T(128)S(6)} %copy.11.hlen_hbm, ...), custom_call_target="tpu_custom_call" | custom-call | tf_op jit(solution)/shard_map/pallas_call | solution.py:405
  47.4 0.8 %copy.10 = bf16[256,1024]{1,0:T(8,128)(2,1)} copy(bf16[256,1024]{1,0:T(8,128)(2,1)S(1)} %shard_map.82) | data formatting | bytes 1048576

commit v5 on v4

--- a/solution.py
+++ b/solution.py
@@ -245,8 +245,6 @@
 
     pass_kv(1)
     pass_q(1)
-    for d in near:
-        pass_k(d)
     for load in loads[4:7]:
         load.wait()
 
@@ -256,7 +254,10 @@
         own_v[part, :, ds] = silu(jnp.dot(n_v[...], win_v[part], preferred_element_type=F32)).astype(BF)
         return 0
 
-    lax.fori_loop(0, 3, rest, 0)
+    lax.fori_loop(0, 2, rest, 0)
+    for d in near:
+        pass_k(d)
+    lax.fori_loop(2, 3, rest, 0)
     for h in range(HEADS):
         ds = pl.ds(h * HD, HD)
         dot = jnp.sum(own_v[2, :, ds].astype(F32) * own_v[3, :, ds].astype(F32), axis=-1, keepdims=True)
@@ -291,26 +292,32 @@
             pass_kv(6)
             pass_kv(7)
 
-        @pl.when(n == 6)
+        gr = (n + 2 - 2 * (n // 4)) % 4
+        hf = n // 4
+        events = pl.ds(pl.multiple_of(hf * 6 * ROWS, 6 * ROWS), 6 * ROWS)
+        acc[hf, group(gr), :] = attend(group(gr), events)
+        return 0
+
+    lax.fori_loop(0, 6, early, 0)
+
+    def partner_rows(m, _):
+        @pl.when(m == 0)
         def _():
             await_q(10)
             await_q(11)
 
-        @pl.when(n == 7)
+        @pl.when(m == 1)
         def _():
             pass_q(6)
             pass_q(7)
             await_q(12)
             await_q(13)
 
-        last = n // 6
-        gr = (1 - last) * ((n + 2 - 2 * (n // 4)) % 4) + last * (1 + n // 2)
-        hf = (1 - last) * (n // 4) + last * (n % 2)
-        events = pl.ds(pl.multiple_of(hf * 6 * ROWS, 6 * ROWS), 6 * ROWS)
-        acc[hf, group(gr), :] = attend(group(gr), events)
-        return 0
-
-    lax.fori_loop(0, 10, early, 0)
+        acc[0, group(4 + m), :] = attend(group(4 + m), pl.ds(0, 12 * ROWS))
+        acc[1, group(4 + m), :] = jnp.zeros((2 * ROWS, HD), F32)
+        return 0
+
+    lax.fori_loop(0, 2, partner_rows, 0)
 
     for d in range(1, 4):
         pass_w(d)
@@ -385,16 +392,11 @@
     attn = attn_v[0].astype(F32) + attn_v[1].astype(F32) + self_v[...]
     n_v[...] = (layer_norm(attn) * own_v[0].astype(F32)).astype(BF)
 
-    def out_piece(p, _):
-        ds = pl.ds(pl.multiple_of(p * 512, 512), 512)
-        mixed = x_v[:, ds].astype(F32) + jnp.dot(n_v[...], wout_v[:, ds], preferred_element_type=F32)
-        for i in range(ROWS // PANEL):
-            number = pmap_ref[i] * PANEL + lax.broadcasted_iota(jnp.int32, (PANEL, 512), 0)
-            keep = mixed[i * PANEL : (i + 1) * PANEL]
-            out_ref[pl.ds(i * PANEL, PANEL), ds] = jnp.where(number < cnt_ref[0], keep, 0.0).astype(BF)
-        return 0
-
-    lax.fori_loop(0, 2, out_piece, 0)
+    mixed = x_v[...].astype(F32) + jnp.dot(n_v[...], wout_v[...], preferred_element_type=F32)
+    for i in range(ROWS // PANEL):
+        number = pmap_ref[i] * PANEL + lax.broadcasted_iota(jnp.int32, (PANEL, D), 0)
+        keep = mixed[i * PANEL : (i + 1) * PANEL]
+        out_ref[pl.ds(i * PANEL, PANEL), :] = jnp.where(number < cnt_ref[0], keep, 0.0).astype(BF)
 
     for copy in sends:
         copy().wait_send()

time: 48.6 us -> 47.3 us (0.973)
  Pallas kernels: 46.1 us -> 44.9 us
    pallas_call x1, Pallas kernels: 46.1 us -> 44.9 us  [per_device(): pl.pallas_call(kernel, out_shape=pltpu.VMEM((ROWS, D), BF), in_specs=[pl....]
where the time goes in v5:
time: 47.3 us; the launch traced here: 47 us
  Pallas kernels  44.9 us (95%)
  between operations  1.3 us (3%)
  local copies, waits for them, and re-layouts  0.8 us (2%)
    pallas_call x1, Pallas kernels, per_device(): pl.pallas_call(kernel, out_shape=pltpu.VMEM((ROWS, D), BF), in_specs=[pl....  44.9 us

profile of v5, /device:TPU:1, one launch (start us, length us, event | category | flops | bytes accessed | tf_op | source)
XLA Modules:
  0.0 47.0 jit_solution(3645149127728601248)
XLA Ops:
  1.3 44.9 %shard_map.82 = bf16[256,1024]{1,0:T(8,128)(2,1)S(1)} custom-call(bf16[256,1024]{1,0:T(8,128)(2,1)} %x_hbm.1, bf16[1024,4096]{1,0:T(8,128)(2,1)} %win_hbm.1, bf16[256,1024]{1,0:T(8,128)(2,1)} %wout_hbm.1, bf16[1,256,1024]{2,1,0:T(8,128)(2,1)} %hk_hbm.1, bf16[1,256,1024]{2,1,0:T(8,128)(2,1)} %hv_hbm.1, s32[1]{0:T(128)S(6)} %copy.11.hlen_hbm, ...), custom_call_target="tpu_custom_call" | custom-call | tf_op jit(solution)/shard_map/pallas_call | solution.py:407
  46.2 0.8 %copy.10 = bf16[256,1024]{1,0:T(8,128)(2,1)} copy(bf16[256,1024]{1,0:T(8,128)(2,1)S(1)} %shard_map.82) | data formatting | bytes 1048576

commit v6 on v5

--- a/solution.py
+++ b/solution.py
@@ -231,10 +231,10 @@
     loads[3].wait()
     own_v[2] = silu(jnp.dot(n_v[...], win_v[2], preferred_element_type=F32)).astype(BF)
     q_all[qs(0), :] = own_v[2, :, cols(head)]
+    send_q(1)
+    pass_q(0)
     for d in near:
         send_q(d)
-    send_q(1)
-    pass_q(0)
     for d in (6, 7):
         send_k(d)
         send_v(d)
@@ -337,9 +337,9 @@
     late = pl.ds(12 * ROWS, 4 * ROWS)
 
     def finish(m, _):
-        gr = (m + 4) % 6
-        osend[group(gr), :] = (acc[0, group(gr), :] + acc[1, group(gr), :] + attend(group(gr), late)).astype(BF)
-        for i, ds in enumerate(((10, 11), (12, 13), (2, 3), (4, 5))):
+        rows = pl.ds(pl.multiple_of((1 - m) * 8 * ROWS, 8 * ROWS), 4 * ROWS)
+        osend[rows, :] = (acc[0, rows, :] + acc[1, rows, :] + attend(rows, late)).astype(BF)
+        for i, ds in enumerate(((10, 11, 12, 13), (2, 3, 4, 5))):
 
             @pl.when(m == i)
             def _():
@@ -348,7 +348,7 @@
 
         return 0
 
-    lax.fori_loop(0, 4, finish, 0)
+    lax.fori_loop(0, 2, finish, 0)
 
     def whole(m, _):
         osend[group(7 - m), :] = attend(group(7 - m), pl.ds(0, 16 * ROWS)).astype(BF)

time: 47.3 us -> 47.1 us (level)
  no operation moved by 1% of the time
where the time goes in v6:
time: 47.1 us; the launch traced here: 46.6 us
  Pallas kernels  44.5 us (94%)
  between operations  1.3 us (3%)
  local copies, waits for them, and re-layouts  0.8 us (2%)
    pallas_call x1, Pallas kernels, per_device(): pl.pallas_call(kernel, out_shape=pltpu.VMEM((ROWS, D), BF), in_specs=[pl....  44.5 us

profile of v6, /device:TPU:1, one launch (start us, length us, event | category | flops | bytes accessed | tf_op | source)
XLA Modules:
  0.0 46.6 jit_solution(3241512012407715028)
XLA Ops:
  1.3 44.5 %shard_map.82 = bf16[256,1024]{1,0:T(8,128)(2,1)S(1)} custom-call(bf16[256,1024]{1,0:T(8,128)(2,1)} %x_hbm.1, bf16[1024,4096]{1,0:T(8,128)(2,1)} %win_hbm.1, bf16[256,1024]{1,0:T(8,128)(2,1)} %wout_hbm.1, bf16[1,256,1024]{2,1,0:T(8,128)(2,1)} %hk_hbm.1, bf16[1,256,1024]{2,1,0:T(8,128)(2,1)} %hv_hbm.1, s32[1]{0:T(128)S(6)} %copy.11.hlen_hbm, ...), custom_call_target="tpu_custom_call" | custom-call | tf_op jit(solution)/shard_map/pallas_call | solution.py:407
  45.8 0.8 %copy.10 = bf16[256,1024]{1,0:T(8,128)(2,1)} copy(bf16[256,1024]{1,0:T(8,128)(2,1)S(1)} %shard_map.82) | data formatting | bytes 1048576

commit v7 on v6

--- a/solution.py
+++ b/solution.py
@@ -389,14 +389,15 @@
         h = peer(d % 8)[1]
         remote(osend.at[qs(d)], attn_v.at[d // 8, :, cols(h)], a_snd.at[d], a_rcv.at[d], event_partner).wait_recv()
 
-    attn = attn_v[0].astype(F32) + attn_v[1].astype(F32) + self_v[...]
-    n_v[...] = (layer_norm(attn) * own_v[0].astype(F32)).astype(BF)
-
-    mixed = x_v[...].astype(F32) + jnp.dot(n_v[...], wout_v[...], preferred_element_type=F32)
-    for i in range(ROWS // PANEL):
-        number = pmap_ref[i] * PANEL + lax.broadcasted_iota(jnp.int32, (PANEL, D), 0)
-        keep = mixed[i * PANEL : (i + 1) * PANEL]
-        out_ref[pl.ds(i * PANEL, PANEL), :] = jnp.where(number < cnt_ref[0], keep, 0.0).astype(BF)
+    for lo in range(0, ROWS, 128):
+        rows = pl.ds(lo, 128)
+        attn = attn_v[0, rows].astype(F32) + attn_v[1, rows].astype(F32) + self_v[rows]
+        n_v[rows] = (layer_norm(attn) * own_v[0, rows].astype(F32)).astype(BF)
+        mixed = x_v[rows].astype(F32) + jnp.dot(n_v[rows], wout_v[...], preferred_element_type=F32)
+        for i in range(128 // PANEL):
+            number = pmap_ref[lo // PANEL + i] * PANEL + lax.broadcasted_iota(jnp.int32, (PANEL, D), 0)
+            keep = mixed[i * PANEL : (i + 1) * PANEL]
+            out_ref[pl.ds(lo + i * PANEL, PANEL), :] = jnp.where(number < cnt_ref[0], keep, 0.0).astype(BF)
 
     for copy in sends:
         copy().wait_send()

time: 47.1 us -> 47 us (level)
  no operation moved by 1% of the time
where the time goes in v7:
time: 47 us; the launch traced here: 46.6 us
  Pallas kernels  44.5 us (95%)
  between operations  1.3 us (3%)
  local copies, waits for them, and re-layouts  0.8 us (2%)
    pallas_call x1, Pallas kernels, per_device(): pl.pallas_call(kernel, out_shape=pltpu.VMEM((ROWS, D), BF), in_specs=[pl....  44.5 us

profile of v7, /device:TPU:1, one launch (start us, length us, event | category | flops | bytes accessed | tf_op | source)
XLA Modules:
  0.0 46.6 jit_solution(488747137769070031)
XLA Ops:
  1.3 44.5 %shard_map.82 = bf16[256,1024]{1,0:T(8,128)(2,1)S(1)} custom-call(bf16[256,1024]{1,0:T(8,128)(2,1)} %x_hbm.1, bf16[1024,4096]{1,0:T(8,128)(2,1)} %win_hbm.1, bf16[256,1024]{1,0:T(8,128)(2,1)} %wout_hbm.1, bf16[1,256,1024]{2,1,0:T(8,128)(2,1)} %hk_hbm.1, bf16[1,256,1024]{2,1,0:T(8,128)(2,1)} %hv_hbm.1, s32[1]{0:T(128)S(6)} %copy.11.hlen_hbm, ...), custom_call_target="tpu_custom_call" | custom-call | tf_op jit(solution)/shard_map/pallas_call | solution.py:408
  45.8 0.8 %copy.10 = bf16[256,1024]{1,0:T(8,128)(2,1)} copy(bf16[256,1024]{1,0:T(8,128)(2,1)S(1)} %shard_map.82) | data formatting | bytes 1048576
